TPU v7x, 256 devices: a whole 4x4x8 slice. The times are simulated.
256 devices in a mesh: gx: 8 (over z_lo, core), gy: 8 (over x, z_hi), gz: 4 (over y).
Axes of the slice: x: 4, y: 4, z: 8 (z_hi: 2, z_lo: 4; z = z_hi * 4 + z_lo), core: 2. Of those that a mesh axis runs over, the one named last changes fastest.
Arguments:
- inputs: bfloat16 [2048, 8192], P('gx', ('gy', 'gz')), may hold values from -6 to 6
- hidden_grad: bfloat16 [2048, 14336], P(('gx', 'gy'), 'gz'), may hold values from -6 to 6
- gate_pre: bfloat16 [2048, 14336], P(('gx', 'gy'), 'gz'), may hold values from -8 to 8
- up_pre: bfloat16 [2048, 14336], P(('gx', 'gy'), 'gz'), may hold values from -6 to 6
- gate_weight: bfloat16 [8192, 14336], P(('gy', 'gx'), 'gz'), may hold values from -0.0625 to 0.0625
- up_weight: bfloat16 [8192, 14336], P(('gy', 'gx'), 'gz'), may hold values from -0.0625 to 0.0625
Outputs:
- input_grad: bfloat16 [2048, 8192], P('gx', ('gy', 'gz'))
- gate_weight_grad: bfloat16 [8192, 14336], P(('gy', 'gx'), 'gz')
- up_weight_grad: bfloat16 [8192, 14336], P(('gy', 'gx'), 'gz')
All inputs are finite; a program needn't handle non-finite values.
Results may differ from a plain program's by a relative error of at most 0.019.
Values may be sent and summed in bfloat16 or wider, within the bound.
A program may use at most 128 MiB of HBM per device.

v0:
```python
import math

import jax
import jax.numpy as jnp
from jax import lax
from jax.sharding import PartitionSpec as P


def hidden_terms(hidden_grad, gate_pre, up_pre):
    incoming = hidden_grad.astype(jnp.float32)
    gating = gate_pre.astype(jnp.float32)
    upper = up_pre.astype(jnp.float32)
    squash = jax.nn.sigmoid(gating)
    gate_grad = (incoming * upper * squash * (1.0 + gating * (1.0 - squash))).astype(jnp.bfloat16)
    up_grad = (incoming * gating * squash).astype(jnp.bfloat16)
    return (gate_grad, up_grad)


def left_product(rows_all, gathered):
    return lax.dot_general(
        rows_all, gathered, (((0,), (0,)), ((), ())), preferred_element_type=jnp.float32
    )


def right_product(gathered, piece):
    return lax.dot_general(
        gathered, piece, (((1,), (1,)), ((), ())), preferred_element_type=jnp.float32
    )


def body(inputs, hidden_grad, gate_pre, up_pre, gate_weight, up_weight):
    rows_all = lax.all_gather(inputs, "gz", axis=1, tiled=True)
    gate_grad, up_grad = hidden_terms(hidden_grad, gate_pre, up_pre)
    hidden_width = gate_weight.shape[1]
    factor = 1.0 / math.sqrt(inputs.shape[0] * lax.axis_size("gx"))
    gate_gathered = lax.all_gather(gate_grad, "gy", axis=0, tiled=True)
    up_gathered = lax.all_gather(up_grad, "gy", axis=0, tiled=True)
    both_gathered = jnp.concatenate([gate_gathered, up_gathered], axis=1)
    summed = lax.psum_scatter(
        left_product(rows_all, both_gathered).astype(jnp.bfloat16),
        "gx",
        scatter_dimension=0,
        tiled=True,
    ).astype(jnp.float32)
    gate_weight_grad = (summed[:, :hidden_width] * factor).astype(jnp.bfloat16)
    up_weight_grad = (summed[:, hidden_width:] * factor).astype(jnp.bfloat16)
    gate_part = right_product(gate_gathered, lax.all_gather(gate_weight, "gx", axis=0, tiled=True))
    up_part = right_product(up_gathered, lax.all_gather(up_weight, "gx", axis=0, tiled=True))
    partial_sum = gate_part + up_part
    input_grad = lax.psum_scatter(
        partial_sum.astype(jnp.bfloat16), "gz", scatter_dimension=1, tiled=True
    )
    return (input_grad, gate_weight_grad, up_weight_grad)


def solution(mesh):
    placed = (
        P("gx", ("gy", "gz")),
        P(("gx", "gy"), "gz"),
        P(("gx", "gy"), "gz"),
        P(("gx", "gy"), "gz"),
        P(("gy", "gx"), "gz"),
        P(("gy", "gx"), "gz"),
    )
    return jax.shard_map(
        body,
        mesh=mesh,
        in_specs=placed,
        out_specs=(P("gx", ("gy", "gz")), P(("gy", "gx"), "gz"), P(("gy", "gx"), "gz")),
        check_vma=False,
    )
```

profile of v0, /device:TPU:2, one launch (start us, length us, event | category | flops | bytes accessed | tf_op | source)
XLA Modules:
  0.0 512.0 jit_solution(13301961370336515348)
XLA Ops:
  7.2 0.0 all-gather.9.cloned.1.call-start
  7.2 2.2 fusion.14
  9.4 0.0 all-gather.9.cloned.1.call-update
  9.4 0.0 all-gather.5.cloned.1.call-start
  9.4 0.7 all-gather.5.cloned.1.call-update
  10.2 0.0 all-gather.7.cloned.1.call-start
  10.2 0.7 all-gather.7.cloned.1.call-update
  10.9 0.0 all-gather.11.cloned.1.call-start
  10.9 0.5 all-gather.11.cloned.1.call-update
  11.5 0.0 reduce-scatter.7.cloned.1.call-start
  11.5 13.5 %all_gather.19 = bf16[256,1024]{1,0:T(8,128)(2,1)S(1)} all-gather(bf16[256,256]{1,0:T(8,128)(2,1)} %param.6), channel_id=1, replica_groups=mesh['gx'=8,'gy'=8,'gz'=4] {'gz'}, dimensions={1}, use_global_device_ids=true | all-gather | bytes 655360 | tf_op jit(solution)/shard_map/all_gather | solution.py:32
  25.0 61.5 %all-gather.9.cloned.1.call-done = bf16[256,3584]{1,0:T(8,128)(2,1)} async-done(((bf16[32,3584]{1,0:T(8,128)(2,1)}), bf16[256,3584]{1,0:T(8,128)(2,1)}) %all-gather.9.cloned.1.call-update) | async-done | bytes 1835024 | tf_op jit(solution)/shard_map/all_gather | solution.py:37
  86.5 71.4 %all-gather.5.cloned.1.call-done = bf16[256,3584]{1,0:T(8,128)(2,1)} async-done(((bf16[32,3584]{1,0:T(8,128)(2,1)}), bf16[256,3584]{1,0:T(8,128)(2,1)}) %all-gather.5.cloned.1.call-update) | async-done | bytes 1835024 | tf_op jit(solution)/shard_map/all_gather | solution.py:36
  157.9 9.7 %convert_bitcast_fusion = bf16[1024,7168]{0,1:T(8,128)(2,1)} fusion(bf16[256,1024]{1,0:T(8,128)(2,1)S(1)} %all_gather.19, bf16[256,3584]{1,0:T(8,128)(2,1)} %all-gather.9.cloned.1.call-done, bf16[256,3584]{1,0:T(8,128)(2,1)} %all-gather.5.cloned.1.call-done), kind=kOutput, calls=%fused_computation | convolution fusion | flops 3772776448 | bytes 18874368 | tf_op jit(solution)/shard_map/dot_general | solution.py:20
  167.6 18.3 %copy.13 = bf16[1024,7168]{1,0:T(8,128)(2,1)} copy(bf16[1024,7168]{0,1:T(8,128)(2,1)} %convert_bitcast_fusion) | data formatting | bytes 29360128
  185.9 0.0 reduce-scatter.7.cloned.1.call-update
  185.9 0.0 copy-start
  185.9 0.0 reduce-scatter.5.cloned.1.call-start
  186.0 53.8 %all-gather.7.cloned.1.call-done = bf16[1024,3584]{1,0:T(8,128)(2,1)} async-done(((bf16[128,3584]{1,0:T(8,128)(2,1)}), bf16[1024,3584]{1,0:T(8,128)(2,1)}) %all-gather.7.cloned.1.call-update) | async-done | bytes 7340048 | tf_op jit(solution)/shard_map/all_gather | solution.py:47
  239.8 5.7 %fusion.16 = f32[256,1024]{1,0:T(8,128)S(1)} fusion(bf16[256,3584]{1,0:T(8,128)(2,1)} %all-gather.5.cloned.1.call-done, bf16[1024,3584]{1,0:T(8,128)(2,1)} %all-gather.7.cloned.1.call-done), kind=kOutput, calls=%fused_computation.24 | convolution fusion | flops 1879048192 | bytes 10223616 | tf_op jit(solution)/shard_map/dot_general | solution.py:26
  245.5 78.7 %all-gather.11.cloned.1.call-done = bf16[1024,3584]{1,0:T(8,128)(2,1)} async-done(((bf16[128,3584]{1,0:T(8,128)(2,1)}), bf16[1024,3584]{1,0:T(8,128)(2,1)}) %all-gather.11.cloned.1.call-update) | async-done | bytes 7340048 | tf_op jit(solution)/shard_map/all_gather | solution.py:48
  324.3 0.0 copy-done
  324.3 6.0 %fusion.5 = bf16[256,1024]{1,0:T(8,128)(2,1)} fusion(f32[256,1024]{1,0:T(8,128)S(1)} %fusion.16, bf16[256,3584]{1,0:T(8,128)(2,1)S(1)} %copy-done, bf16[1024,3584]{1,0:T(8,128)(2,1)} %all-gather.11.cloned.1.call-done), kind=kOutput, calls=%fused_computation.9 | convolution fusion | flops 1879572480 | bytes 10747904 | tf_op jit(solution)/shard_map/dot_general | solution.py:26
  330.2 0.0 reduce-scatter.5.cloned.1.call-update
  330.3 149.4 %reduce-scatter.7.cloned.1.call-done = bf16[128,7168]{1,0:T(8,128)(2,1)} async-done(((bf16[1024,7168]{1,0:T(8,128)(2,1)}), bf16[128,7168]{1,0:T(8,128)(2,1)}) %reduce-scatter.7.cloned.1.call-update) | async-done | bytes 1835024
  479.6 3.3 copy.14
  482.9 0.2 convert_element_type.41
  483.2 0.4 fusion.3
  483.6 1.3 copy.12
  484.8 1.3 copy.11
  486.1 19.1 %reduce-scatter.5.cloned.1.call-done = bf16[256,256]{1,0:T(8,128)(2,1)} async-done(((bf16[256,1024]{1,0:T(8,128)(2,1)}), bf16[256,256]{1,0:T(8,128)(2,1)}) %reduce-scatter.5.cloned.1.call-update) | async-done | bytes 131088 | tf_op jit(solution)/shard_map/reduce_scatter | solution.py:50
Async XLA Ops:
  7.2 79.3 %all-gather.9.cloned.1.call-start = ((), (), s32[]{:S(2)}) async-start(), calls=%async_computation.4 | async-start | bytes 2064384 | tf_op jit(solution)/shard_map/all_gather | solution.py:37
  9.4 148.5 %all-gather.5.cloned.1.call-start = ((), (), s32[]{:S(2)}) async-start(), calls=%async_computation.2 | async-start | bytes 2064384 | tf_op jit(solution)/shard_map/all_gather | solution.py:36
  10.2 229.6 %all-gather.7.cloned.1.call-start = ((), (), s32[]{:S(2)}) async-start(), calls=%async_computation.3 | async-start | bytes 8257536 | tf_op jit(solution)/shard_map/all_gather | solution.py:47
  10.9 313.4 %all-gather.11.cloned.1.call-start = ((), (), s32[]{:S(2)}) async-start(), calls=%async_computation.5 | async-start | bytes 8257536 | tf_op jit(solution)/shard_map/all_gather | solution.py:48
  11.5 468.2 %reduce-scatter.7.cloned.1.call-start = ((), (), s32[]{:S(2)}) async-start(), calls=%async_computation.7 | async-start | bytes 16515072
  185.9 138.4 %copy-start = (bf16[256,3584]{1,0:T(8,128)(2,1)S(1)}, bf16[256,3584]{1,0:T(8,128)(2,1)}, u32[]{:S(2)}) copy-start(bf16[256,3584]{1,0:T(8,128)(2,1)} %all-gather.9.cloned.1.call-done) | copy-start | bytes 5505028
  185.9 319.3 %reduce-scatter.5.cloned.1.call-start = ((), (), s32[]{:S(2)}) async-start(), calls=%async_computation.6 | async-start | bytes 655360 | tf_op jit(solution)/shard_map/reduce_scatter | solution.py:50
Sparse Core Ops, SparseCore 0:
  11.2 75.2 all-gather.8
  89.7 68.1 all-gather.4
  159.7 80.0 all-gather.6
  241.4 82.7 all-gather.10
  326.7 152.8 reduce-scatter.6
  482.6 22.5 reduce-scatter.4
where the time goes:
time: 513 us; the launch traced here: 512 us
  waiting for transfers between devices  436 us (85%)
  local copies, waits for them, and re-layouts  24.2 us (5%)
  matrix products  21.4 us (4%)
  between operations  14.2 us (3%)
  blocking collectives  13.5 us (3%)
    unnamed x7, waiting for transfers between devices  151 us
    all_gather x1, waiting for transfers between devices, body(): lax.all_gather(up_weight, 'gx', axis=0, tiled=True)  78.7 us
    all_gather x1, waiting for transfers between devices, body(): gate_gathered = lax.all_gather(gate_grad, 'gy', axis=0, tiled=True)  71.4 us
    all_gather x1, waiting for transfers between devices, body(): up_gathered = lax.all_gather(up_grad, 'gy', axis=0, tiled=True)  61.5 us
    all_gather x1, waiting for transfers between devices, body(): lax.all_gather(gate_weight, 'gx', axis=0, tiled=True)  53.8 us
    unnamed x6, local copies, waits for them, and re-layouts  24.2 us
    reduce_scatter x1, waiting for transfers between devices, body(): lax.psum_scatter(partial_sum.astype(jnp.bfloat16), 'gz', scatter_dimensio...  19.1 us
    all_gather x1, blocking collectives, body(): rows_all = lax.all_gather(inputs, 'gz', axis=1, tiled=True)  13.5 us
  transfers between devices with their start and end apart: 6, of which 6 were waited for; matrix products, arithmetic and copies ran while one was open for 9% of the time, Pallas kernels for 0%

commit v1 on v0

v1 whole, which is shorter than its diff:
```python
import functools
import math

import jax
import jax.numpy as jnp
from jax import lax
from jax.experimental import pallas as pl
from jax.experimental.pallas import tpu as pltpu
from jax.sharding import PartitionSpec as P

MESH = pl.DeviceIdType.MESH
BF16, F32 = jnp.bfloat16, jnp.float32

NX, NY, NZH, NZL = 4, 4, 2, 4
NZ = NZH * NZL


def aligned(index, step, size):
    return pl.ds(pl.multiple_of(index * step, step), size)


def kernel(
    factor,
    x_ref, h_ref, g_ref, u_ref, wg_ref, wu_ref,
    dx_ref, dwg_ref, dwu_ref,
    g0, gbuf, wbuf, xt0, xbuf, dxs, dxr, dxp, dxq, dwt, dws, dwr, dwf,
    ga_s, ga_r, gr_s, gr_r, wa_s, wa_r, wc_s, wc_r, xa_s, xa_r, xb_s, xb_r,
    dy_s, dy_r, dq_s, dq_r, ec_s, ec_r, eo_s, eo_r,
):
    gx, gy, gz = lax.axis_index("gx"), lax.axis_index("gy"), lax.axis_index("gz")
    x, zh, y, zl, c = gy // NZH, gy % NZH, gz, gx // 2, gx % 2
    z = zh * NZL + zl
    rows = h_ref.shape[0]
    fq = h_ref.shape[1] // NX
    wr = wg_ref.shape[0]
    dc = 2 * wr
    shard = NX * rows
    blk = NZH * shard
    half = shard // 2
    w_refs, dw_refs = (wg_ref, wu_ref), (dwg_ref, dwu_ref)

    def dev(xx, yy, zz, cc):
        return ((zz % NZL) * 2 + cc, xx * NZH + zz // NZL, yy)

    def remote(src, dst, ss, rs, to):
        return pltpu.make_async_remote_copy(
            src_ref=src, dst_ref=dst, send_sem=ss, recv_sem=rs, device_id=to, device_id_type=MESH
        )

    here = dev(x, y, z, c)
    pair = dev(x, y, z, 1 - c)
    xs = [(x + k) % NX for k in range(NX)]
    ys = [(y + k) % NY for k in range(NY)]
    up, down = dev(x, y, (z + 1) % NZ, c), dev(x, y, (z + NZ - 1) % NZ, c)
    swapped = [dev(xs[k], zl, zh * NZL + y, c) for k in range(NX)]
    on_diag = y == zl

    def landed(ref, sem):
        remote(ref, ref, sem, sem, pair).wait_recv()

    def sent(ref, sem):
        remote(ref, ref, sem, sem, pair).wait_send()

    barrier = pltpu.get_barrier_semaphore()

    def greet(to):
        pl.semaphore_signal(barrier, inc=1, device_id=to, device_id_type=MESH)

    for k in range(1, NX):
        greet(dev(xs[k], y, z, c))
    for k in range(1, NY):
        greet(dev(x, ys[k], z, c))
    greet(up)
    greet(down)
    greet(pair)

    @pl.when(on_diag)
    def _():
        pl.semaphore_wait(barrier, (NX - 1) + (NY - 1) + 3)

    @pl.when(jnp.logical_not(on_diag))
    def _():
        for k in range(NX):
            greet(swapped[k])
        pl.semaphore_wait(barrier, (NX - 1) + (NY - 1) + 3 + NX)

    for q in range(NX):
        part = slice(q * fq, (q + 1) * fq)
        hh = h_ref[:, part].astype(F32)
        gg = g_ref[:, part].astype(F32)
        uu = u_ref[:, part].astype(F32)
        sq = jax.nn.sigmoid(gg)
        g0[q, 0] = (hh * uu * sq * (1.0 + gg * (1.0 - sq))).astype(BF16)
        g0[q, 1] = (hh * gg * sq).astype(BF16)

    def place(zz):
        zz = zz % NZ
        return (zz % NZL) * NZH + zz // NZL

    mine = place(z)
    g_mine = gbuf.at[:, mine, aligned(x, rows, rows), :]
    pltpu.make_async_copy(g0.at[x], g_mine, ga_r.at[x]).start()
    for k in range(1, NX):
        remote(g0.at[xs[k]], g_mine, ga_s.at[k], ga_r.at[x], dev(xs[k], y, z, c)).start()

    xin = x_ref[...].astype(F32)
    xp = jnp.concatenate(
        [xin[(i * NZH + j) * rows:(i * NZH + j + 1) * rows] for j in range(NZH) for i in range(NX)], axis=0
    )
    xt0[...] = xp.T.astype(BF16)
    x_dst = xbuf.at[aligned(x, dc, dc), aligned(zl, blk, blk)]

    def x_send(k):
        return remote(xt0, x_dst, xa_s.at[k], xa_r.at[x], swapped[k])

    for k in range(1, NX):
        x_send(k).start()

    @pl.when(on_diag)
    def _():
        pltpu.make_async_copy(xt0, x_dst, xa_r.at[x]).start()

    @pl.when(jnp.logical_not(on_diag))
    def _():
        x_send(0).start()

    def w_src(gu, q):
        return w_refs[gu].at[:, aligned(q, fq, fq)]

    def w_rows(gu, i, cc):
        return wbuf.at[gu, aligned(i * 2 + cc, wr, wr), :]

    def w_send(gu, k):
        return remote(w_src(gu, xs[k]), w_rows(gu, x, c), wa_s.at[gu, k], wa_r.at[gu, x], dev(xs[k], y, z, c))

    for gu in range(2):
        pltpu.make_async_copy(w_src(gu, x), w_rows(gu, x, c), wa_r.at[gu, x]).start()
        for k in range(1, NX):
            w_send(gu, k).start()

    def w_forward(gu):
        for i in range(NX):
            landed(w_rows(gu, i, c), wa_r.at[gu, i])
            remote(w_rows(gu, i, c), w_rows(gu, i, c), wc_s.at[gu, i], wc_r.at[gu, i], pair).start()

    def ring_ref(gu, zz, part):
        return gbuf.at[gu, place(zz), pl.ds(part * half, half), :]

    def ring_send(gu, d, s, part):
        ref = ring_ref(gu, z + (NZ - s if d == 0 else s), part)
        return remote(ref, ref, gr_s.at[gu, d, s, part], gr_r.at[gu, d, s, part], up if d == 0 else down)

    def ring_landed(gu, d, s, part):
        landed(ring_ref(gu, z + (NZ - 1 - s if d == 0 else 1 + s), part), gr_r.at[gu, d, s, part])

    def part_of(d, j):
        return j if d == 0 else 1 - j

    last = NZ // 2 - 1

    def ring_first(gu):
        for j in range(2):
            for d in range(2):
                ring_send(gu, d, 0, part_of(d, j)).start()

    def ring_step(gu, s):
        for j in range(2 if s < last else 1):
            for d in range(2):
                ring_landed(gu, d, s - 1, part_of(d, j))
                ring_send(gu, d, s, part_of(d, j)).start()

    def ring_end(gu):
        for d in range(2):
            ring_landed(gu, d, last - 1, part_of(d, 1))
        for d in range(2):
            ring_landed(gu, d, last, part_of(d, 0))

    for i in range(NX):
        landed(gbuf.at[:, mine, pl.ds(i * rows, rows), :], ga_r.at[i])
    ring_first(0)

    for i in range(NX):
        landed(xbuf.at[pl.ds(i * dc, dc), aligned(y, blk, blk)], xa_r.at[i])
    x_block = xbuf.at[:, aligned(y, blk, blk)]
    for k in range(1, NY):
        remote(x_block, x_block, xb_s.at[k], xb_r.at[y], dev(x, ys[k], z, c)).start()

    ring_step(0, 1)
    w_forward(0)
    ring_step(0, 2)
    ring_step(0, 3)
    ring_first(1)
    w_forward(1)

    def dw_out(gu, q):
        return dw_refs[gu].at[:, aligned(q, fq, fq)]

    def dw_send(gu, k):
        return remote(dwf.at[gu, xs[k]], dw_out(gu, x), eo_s.at[gu, k], eo_r.at[gu, x], dev(xs[k], y, z, c))

    def dw_pair(gu, i):
        return remote(dws.at[gu, i], dwr.at[gu, i], ec_s.at[gu, i], ec_r.at[gu, i], pair)

    def dw_compute(gu):
        tokens = gbuf.at[gu]

        @pl.loop(0, NX)
        def _(i):
            lhs = xbuf[aligned(i, dc, dc), :]
            rhs = tokens[...].reshape(NZ * shard, fq)
            dwt[gu, i] = jnp.dot(lhs, rhs, preferred_element_type=F32)
            dws[gu, i] = dwt[gu, i, aligned(1 - c, wr, wr), :].astype(BF16)
            dw_pair(gu, i).start()

    def dw_finish(gu):
        for k in range(NX - 1, -1, -1):
            i = xs[k]
            landed(dwr.at[gu, i], ec_r.at[gu, i])
            total = dwt[gu, i, aligned(c, wr, wr), :] + dwr[gu, i].astype(F32)
            dwf[gu, i] = (total * factor).astype(BF16)
            if k:
                dw_send(gu, k).start()
            else:
                pltpu.make_async_copy(dwf.at[gu, i], dw_out(gu, x), eo_r.at[gu, x]).start()

    def dx_parts(p, d_zh, d_zl):
        return dxs.at[p], dxr.at[y, d_zh]

    def dx_shard(zz):
        zz = zz % NZ
        p, j, owner = place(zz), zz // NZL, zz % NZL

        @pl.loop(0, NX)
        def _(i):
            columns = aligned(i, dc, dc)
            total = lax.dot_general(
                gbuf[0, p], wbuf[0, columns, :], (((1,), (1,)), ((), ())), preferred_element_type=F32
            ) + lax.dot_general(
                gbuf[1, p], wbuf[1, columns, :], (((1,), (1,)), ((), ())), preferred_element_type=F32
            )
            dxs[p, :, columns] = total.astype(BF16)

        @pl.when(owner == y)
        def _():
            pltpu.make_async_copy(dxs.at[p], dxr.at[y, j], dy_r.at[y, j]).start()

        @pl.when(owner != y)
        def _():
            remote(dxs.at[p], dxr.at[y, j], dy_s.at[p], dy_r.at[y, j], dev(x, owner, z, c)).start()

    ring_end(0)
    for k in range(1, NY):
        landed(xbuf.at[:, aligned(ys[k], blk, blk)], xb_r.at[ys[k]])
    dw_compute(0)
    ring_step(1, 1)
    dw_finish(0)
    for gu in range(2):
        for i in range(NX):
            landed(w_rows(gu, i, 1 - c), wc_r.at[gu, i])
    dx_shard(z)
    ring_step(1, 2)
    dx_shard(z + NZ - 1)
    dx_shard(z + 1)
    ring_step(1, 3)
    dx_shard(z + NZ - 2)
    dx_shard(z + 2)
    ring_end(1)
    dx_shard(z + NZ - 3)
    dx_shard(z + 3)
    dx_shard(z + 4)
    dw_compute(1)
    dw_finish(1)

    for i in range(NY):
        for j in range(NZH):
            landed(dxr.at[i, j], dy_r.at[i, j])
    for i in range(NX):
        columns = slice(i * dc, (i + 1) * dc)
        total = dxr[0, :, :, columns].astype(F32)
        for k in range(1, NY):
            total = total + dxr[k, :, :, columns].astype(F32)
        dxp[i] = total.astype(BF16)

    def dx_send(k):
        return remote(dxp.at[xs[k]], dxq.at[x], dq_s.at[k], dq_r.at[x], swapped[k])

    for k in range(1, NX):
        dx_send(k).start()

    @pl.when(on_diag)
    def _():
        pltpu.make_async_copy(dxp.at[x], dxq.at[x], dq_r.at[x]).start()

    @pl.when(jnp.logical_not(on_diag))
    def _():
        dx_send(0).start()

    for i in range(NX):
        landed(dxq.at[i], dq_r.at[i])
    for j in range(NZH):
        for i in range(NX):
            part = slice(i * rows, (i + 1) * rows)
            total = dxq[0, j, part, :].astype(F32)
            for k in range(1, NX):
                total = total + dxq[k, j, part, :].astype(F32)
            dx_ref[(i * NZH + j) * rows:(i * NZH + j + 1) * rows, :] = total.astype(BF16)

    for gu in range(2):
        for i in range(NX):
            landed(dw_out(gu, i), eo_r.at[gu, i])
    for k in range(1, NX):
        sent(g0.at[xs[k]], ga_s.at[k])
        sent(xt0, xa_s.at[k])
        sent(x_block, xb_s.at[k])
        sent(dxp.at[xs[k]], dq_s.at[k])
        for gu in range(2):
            sent(w_src(gu, xs[k]), wa_s.at[gu, k])
            sent(dwf.at[gu, xs[k]], eo_s.at[gu, k])

    @pl.when(jnp.logical_not(on_diag))
    def _():
        sent(xt0, xa_s.at[0])
        sent(dxp.at[x], dq_s.at[0])

    for gu in range(2):
        for i in range(NX):
            sent(w_rows(gu, i, c), wc_s.at[gu, i])
            sent(dws.at[gu, i], ec_s.at[gu, i])
        for s in range(last + 1):
            for j in range(2 if s < last else 1):
                for d in range(2):
                    ring_send(gu, d, s, part_of(d, j)).wait_send()
    for p in range(NZ):

        @pl.when(p // NZH != y)
        def _():
            sent(dxs.at[p], dy_s.at[p])


def body(inputs, hidden_grad, gate_pre, up_pre, gate_weight, up_weight):
    rows, width = hidden_grad.shape
    wr = gate_weight.shape[0]
    fq, shard, dc = width // NX, NX * rows, 2 * wr
    tokens, columns = NZ * shard, NX * dc
    factor = 1.0 / math.sqrt(inputs.shape[0] * lax.axis_size("gx"))
    vmem, anywhere = pl.BlockSpec(memory_space=pltpu.VMEM), pl.BlockSpec(memory_space=pl.ANY)
    dma = pltpu.SemaphoreType.DMA
    return pl.pallas_call(
        functools.partial(kernel, factor),
        out_shape=(
            jax.ShapeDtypeStruct(inputs.shape, BF16),
            jax.ShapeDtypeStruct(gate_weight.shape, BF16),
            jax.ShapeDtypeStruct(up_weight.shape, BF16),
        ),
        in_specs=[vmem, vmem, vmem, vmem, anywhere, anywhere],
        out_specs=(vmem, anywhere, anywhere),
        scratch_shapes=[
            pltpu.VMEM((NX, 2, rows, fq), BF16),
            pltpu.VMEM((2, NZ, shard, fq), BF16),
            pltpu.VMEM((2, columns, fq), BF16),
            pltpu.VMEM((dc, NZH * shard), BF16),
            pltpu.VMEM((columns, tokens), BF16),
            pltpu.VMEM((NZ, shard, columns), BF16),
            pltpu.VMEM((NY, NZH, shard, columns), BF16),
            pltpu.VMEM((NX, NZH, shard, dc), BF16),
            pltpu.VMEM((NX, NZH, shard, dc), BF16),
            pltpu.VMEM((2, NX, dc, fq), F32),
            pltpu.VMEM((2, NX, wr, fq), BF16),
            pltpu.VMEM((2, NX, wr, fq), BF16),
            pltpu.VMEM((2, NX, wr, fq), BF16),
            dma((NX,)), dma((NX,)),
            dma((2, 2, NZ // 2, 2)), dma((2, 2, NZ // 2, 2)),
            dma((2, NX)), dma((2, NX)),
            dma((2, NX)), dma((2, NX)),
            dma((NX,)), dma((NX,)),
            dma((NY,)), dma((NY,)),
            dma((NZ,)), dma((NY, NZH)),
            dma((NX,)), dma((NX,)),
            dma((2, NX)), dma((2, NX)),
            dma((2, NX)), dma((2, NX)),
        ],
        compiler_params=pltpu.CompilerParams(
            collective_id=0, has_side_effects=True, vmem_limit_bytes=56 << 20
        ),
        cost_estimate=pl.CostEstimate(
            flops=8 * tokens * columns * fq, bytes_accessed=12 * wr * width, transcendentals=rows * width
        ),
        name="swiglu_backward",
    )(inputs, hidden_grad, gate_pre, up_pre, gate_weight, up_weight)


def solution(mesh):
    placed = (
        P("gx", ("gy", "gz")),
        P(("gx", "gy"), "gz"),
        P(("gx", "gy"), "gz"),
        P(("gx", "gy"), "gz"),
        P(("gy", "gx"), "gz"),
        P(("gy", "gx"), "gz"),
    )
    return jax.shard_map(
        body,
        mesh=mesh,
        in_specs=placed,
        out_specs=(P("gx", ("gy", "gz")), P(("gy", "gx"), "gz"), P(("gy", "gx"), "gz")),
        check_vma=False,
    )
```

time: 513 us -> 148 us (0.29)
  the two profiles are of different devices: /device:TPU:2 before, /device:TPU:113 now
where the time goes in v1:
time: 148 us
  Pallas kernels  142 us (96%)
  local copies, waits for them, and re-layouts  4.74 us (3%)
    pallas_call x1, Pallas kernels, body(): pl.pallas_call(functools.partial(kernel, factor), out_shape=(jax.ShapeDty...  142 us
    unnamed x5, local copies, waits for them, and re-layouts  4.74 us

profile of v1, /device:TPU:113, one launch (start us, length us, event | category | flops | bytes accessed | tf_op | source)
XLA Modules:
  0.0 147.6 jit_solution(2315447184733446730)
XLA Ops:
  0.6 142.3 %swiglu_backward.1 = (bf16[256,256]{1,0:T(8,128)(2,1)}, bf16[128,3584]{1,0:T(8,128)(2,1)}, bf16[128,3584]{1,0:T(8,128)(2,1)}) custom-call(bf16[256,256]{1,0:T(8,128)(2,1)} %x_ref.1, bf16[32,3584]{1,0:T(8,128)(2,1)} %h_ref.1, bf16[32,3584]{1,0:T(8,128)(2,1)} %g_ref.1, bf16[32,3584]{1,0:T(8,128)(2,1)} %u_ref.1, bf16[128,3584]{1,0:T(8,128)(2,1)} %wg_ref.1, ...), custom_call_target="tpu_custom_call" | custom-call | flops 7516192768 | bytes 5505024 | tf_op jit(solution)/shard_map/swiglu_backward/pallas_call | solution.py:348
  142.9 1.6 %copy.12 = bf16[256,256]{1,0:T(8,128)(2,1)} copy(bf16[256,256]{1,0:T(8,128)(2,1)} %get-tuple-element.6) | data formatting | bytes 262144
  144.5 0.0 copy-start
  144.5 2.2 %copy.13 = bf16[128,3584]{1,0:T(8,128)(2,1)} copy(bf16[128,3584]{1,0:T(8,128)(2,1)} %get-tuple-element.7) | data formatting | bytes 1835008
  146.7 0.0 copy-done
  146.7 0.9 copy.14
Async XLA Ops:
  144.5 2.2 %copy-start = (bf16[128,3584]{1,0:T(8,128)(2,1)S(1)}, bf16[128,3584]{1,0:T(8,128)(2,1)}, u32[]{:S(2)}) copy-start(bf16[128,3584]{1,0:T(8,128)(2,1)} %get-tuple-element.8) | copy-start | bytes 2752516

commit v2 on v1

--- a/solution.py
+++ b/solution.py
@@ -23,9 +23,9 @@
     factor,
     x_ref, h_ref, g_ref, u_ref, wg_ref, wu_ref,
     dx_ref, dwg_ref, dwu_ref,
-    g0, gbuf, wbuf, xt0, xbuf, dxs, dxr, dxp, dxq, dwt, dws, dwr, dwf,
-    ga_s, ga_r, gr_s, gr_r, wa_s, wa_r, wc_s, wc_r, xa_s, xa_r, xb_s, xb_r,
-    dy_s, dy_r, dq_s, dq_r, ec_s, ec_r, eo_s, eo_r,
+    g0, gbuf, wbuf, xt0, xbuf, dxs, dxr, dxp, dxq, dxo, dwt, dws, dwr, dwf,
+    ga_s, ga_r, gr_s, gr_r, wa_s, wa_r, wc_s, wc_r, xa_s, xa_r, xb_s, xb_r, xc_s, xc_r,
+    dy_s, dy_r, dq_s, dq_r, do_s, do_r, ec_s, ec_r, eo_s, eo_r,
 ):
     gx, gy, gz = lax.axis_index("gx"), lax.axis_index("gy"), lax.axis_index("gz")
     x, zh, y, zl, c = gy // NZH, gy % NZH, gz, gx // 2, gx % 2
@@ -52,7 +52,7 @@
     xs = [(x + k) % NX for k in range(NX)]
     ys = [(y + k) % NY for k in range(NY)]
     up, down = dev(x, y, (z + 1) % NZ, c), dev(x, y, (z + NZ - 1) % NZ, c)
-    swapped = [dev(xs[k], zl, zh * NZL + y, c) for k in range(NX)]
+    swapped = dev(x, zl, zh * NZL + y, c)
     on_diag = y == zl
 
     def landed(ref, sem):
@@ -80,9 +80,8 @@
 
     @pl.when(jnp.logical_not(on_diag))
     def _():
-        for k in range(NX):
-            greet(swapped[k])
-        pl.semaphore_wait(barrier, (NX - 1) + (NY - 1) + 3 + NX)
+        greet(swapped)
+        pl.semaphore_wait(barrier, (NX - 1) + (NY - 1) + 4)
 
     for q in range(NX):
         part = slice(q * fq, (q + 1) * fq)
@@ -110,19 +109,13 @@
     xt0[...] = xp.T.astype(BF16)
     x_dst = xbuf.at[aligned(x, dc, dc), aligned(zl, blk, blk)]
 
-    def x_send(k):
-        return remote(xt0, x_dst, xa_s.at[k], xa_r.at[x], swapped[k])
-
-    for k in range(1, NX):
-        x_send(k).start()
-
     @pl.when(on_diag)
     def _():
-        pltpu.make_async_copy(xt0, x_dst, xa_r.at[x]).start()
+        pltpu.make_async_copy(xt0, x_dst, xa_r).start()
 
     @pl.when(jnp.logical_not(on_diag))
     def _():
-        x_send(0).start()
+        remote(xt0, x_dst, xa_s, xa_r, swapped).start()
 
     def w_src(gu, q):
         return w_refs[gu].at[:, aligned(q, fq, fq)]
@@ -133,7 +126,7 @@
     def w_send(gu, k):
         return remote(w_src(gu, xs[k]), w_rows(gu, x, c), wa_s.at[gu, k], wa_r.at[gu, x], dev(xs[k], y, z, c))
 
-    for gu in range(2):
+    def w_start(gu):
         pltpu.make_async_copy(w_src(gu, x), w_rows(gu, x, c), wa_r.at[gu, x]).start()
         for k in range(1, NX):
             w_send(gu, k).start()
@@ -163,11 +156,10 @@
             for d in range(2):
                 ring_send(gu, d, 0, part_of(d, j)).start()
 
-    def ring_step(gu, s):
-        for j in range(2 if s < last else 1):
-            for d in range(2):
-                ring_landed(gu, d, s - 1, part_of(d, j))
-                ring_send(gu, d, s, part_of(d, j)).start()
+    def ring_step(gu, s, j):
+        for d in range(2):
+            ring_landed(gu, d, s - 1, part_of(d, j))
+            ring_send(gu, d, s, part_of(d, j)).start()
 
     def ring_end(gu):
         for d in range(2):
@@ -175,22 +167,28 @@
         for d in range(2):
             ring_landed(gu, d, last, part_of(d, 0))
 
-    for i in range(NX):
-        landed(gbuf.at[:, mine, pl.ds(i * rows, rows), :], ga_r.at[i])
-    ring_first(0)
-
-    for i in range(NX):
-        landed(xbuf.at[pl.ds(i * dc, dc), aligned(y, blk, blk)], xa_r.at[i])
-    x_block = xbuf.at[:, aligned(y, blk, blk)]
-    for k in range(1, NY):
-        remote(x_block, x_block, xb_s.at[k], xb_r.at[y], dev(x, ys[k], z, c)).start()
-
-    ring_step(0, 1)
-    w_forward(0)
-    ring_step(0, 2)
-    ring_step(0, 3)
-    ring_first(1)
-    w_forward(1)
+    def x_piece(i, k):
+        return xbuf.at[aligned(i, dc, dc), aligned(k, blk, blk)]
+
+    def x_along_y(i):
+        for k in range(1, NY):
+            remote(x_piece(i, y), x_piece(i, y), xb_s.at[i, k], xb_r.at[i, y], dev(x, ys[k], z, c)).start()
+
+    def x_start():
+        landed(x_piece(x, y), xa_r)
+        for k in range(1, NX):
+            remote(x_piece(x, y), x_piece(x, y), xc_s.at[k], xc_r.at[x], dev(xs[k], y, z, c)).start()
+        x_along_y(x)
+
+    def x_forward():
+        for k in range(1, NX):
+            landed(x_piece(xs[k], y), xc_r.at[xs[k]])
+            x_along_y(xs[k])
+
+    def x_end():
+        for i in range(NX):
+            for k in range(1, NY):
+                landed(x_piece(i, ys[k]), xb_r.at[i, ys[k]])
 
     def dw_out(gu, q):
         return dw_refs[gu].at[:, aligned(q, fq, fq)]
@@ -248,20 +246,39 @@
         def _():
             remote(dxs.at[p], dxr.at[y, j], dy_s.at[p], dy_r.at[y, j], dev(x, owner, z, c)).start()
 
+    def w_end():
+        for gu in range(2):
+            for i in range(NX):
+                landed(w_rows(gu, i, 1 - c), wc_r.at[gu, i])
+
+    for i in range(NX):
+        landed(gbuf.at[:, mine, pl.ds(i * rows, rows), :], ga_r.at[i])
+    ring_first(0)
+    w_start(0)
+    x_start()
+    ring_step(0, 1, 0)
+    ring_step(0, 1, 1)
+    x_forward()
+    w_start(1)
+    ring_step(0, 2, 0)
+    w_forward(0)
+    ring_step(0, 2, 1)
+    ring_step(0, 3, 0)
+    ring_first(1)
     ring_end(0)
-    for k in range(1, NY):
-        landed(xbuf.at[:, aligned(ys[k], blk, blk)], xb_r.at[ys[k]])
+    ring_step(1, 1, 0)
+    ring_step(1, 1, 1)
+    w_forward(1)
+    x_end()
     dw_compute(0)
-    ring_step(1, 1)
+    ring_step(1, 2, 0)
+    w_end()
+    dx_shard(z)
     dw_finish(0)
-    for gu in range(2):
-        for i in range(NX):
-            landed(w_rows(gu, i, 1 - c), wc_r.at[gu, i])
-    dx_shard(z)
-    ring_step(1, 2)
+    ring_step(1, 2, 1)
     dx_shard(z + NZ - 1)
     dx_shard(z + 1)
-    ring_step(1, 3)
+    ring_step(1, 3, 0)
     dx_shard(z + NZ - 2)
     dx_shard(z + 2)
     ring_end(1)
@@ -281,20 +298,9 @@
             total = total + dxr[k, :, :, columns].astype(F32)
         dxp[i] = total.astype(BF16)
 
-    def dx_send(k):
-        return remote(dxp.at[xs[k]], dxq.at[x], dq_s.at[k], dq_r.at[x], swapped[k])
-
+    pltpu.make_async_copy(dxp.at[x], dxq.at[x], dq_r.at[x]).start()
     for k in range(1, NX):
-        dx_send(k).start()
-
-    @pl.when(on_diag)
-    def _():
-        pltpu.make_async_copy(dxp.at[x], dxq.at[x], dq_r.at[x]).start()
-
-    @pl.when(jnp.logical_not(on_diag))
-    def _():
-        dx_send(0).start()
-
+        remote(dxp.at[xs[k]], dxq.at[x], dq_s.at[k], dq_r.at[x], dev(xs[k], y, z, c)).start()
     for i in range(NX):
         landed(dxq.at[i], dq_r.at[i])
     for j in range(NZH):
@@ -303,15 +309,26 @@
             total = dxq[0, j, part, :].astype(F32)
             for k in range(1, NX):
                 total = total + dxq[k, j, part, :].astype(F32)
-            dx_ref[(i * NZH + j) * rows:(i * NZH + j + 1) * rows, :] = total.astype(BF16)
+            dxo[(i * NZH + j) * rows:(i * NZH + j + 1) * rows, :] = total.astype(BF16)
+
+    @pl.when(on_diag)
+    def _():
+        pltpu.make_async_copy(dxo, dx_ref, do_r).start()
+
+    @pl.when(jnp.logical_not(on_diag))
+    def _():
+        remote(dxo, dx_ref, do_s, do_r, swapped).start()
+
+    landed(dx_ref, do_r)
 
     for gu in range(2):
         for i in range(NX):
             landed(dw_out(gu, i), eo_r.at[gu, i])
     for k in range(1, NX):
         sent(g0.at[xs[k]], ga_s.at[k])
-        sent(xt0, xa_s.at[k])
-        sent(x_block, xb_s.at[k])
+        sent(x_piece(x, y), xc_s.at[k])
+        for i in range(NX):
+            sent(x_piece(i, y), xb_s.at[i, k])
         sent(dxp.at[xs[k]], dq_s.at[k])
         for gu in range(2):
             sent(w_src(gu, xs[k]), wa_s.at[gu, k])
@@ -319,8 +336,8 @@
 
     @pl.when(jnp.logical_not(on_diag))
     def _():
-        sent(xt0, xa_s.at[0])
-        sent(dxp.at[x], dq_s.at[0])
+        sent(xt0, xa_s)
+        sent(dxo, do_s)
 
     for gu in range(2):
         for i in range(NX):
@@ -364,6 +381,7 @@
             pltpu.VMEM((NY, NZH, shard, columns), BF16),
             pltpu.VMEM((NX, NZH, shard, dc), BF16),
             pltpu.VMEM((NX, NZH, shard, dc), BF16),
+            pltpu.VMEM((NZH * shard, dc), BF16),
             pltpu.VMEM((2, NX, dc, fq), F32),
             pltpu.VMEM((2, NX, wr, fq), BF16),
             pltpu.VMEM((2, NX, wr, fq), BF16),
@@ -372,10 +390,12 @@
             dma((2, 2, NZ // 2, 2)), dma((2, 2, NZ // 2, 2)),
             dma((2, NX)), dma((2, NX)),
             dma((2, NX)), dma((2, NX)),
+            dma, dma,
+            dma((NX, NY)), dma((NX, NY)),
             dma((NX,)), dma((NX,)),
-            dma((NY,)), dma((NY,)),
             dma((NZ,)), dma((NY, NZH)),
             dma((NX,)), dma((NX,)),
+            dma, dma,
             dma((2, NX)), dma((2, NX)),
             dma((2, NX)), dma((2, NX)),
         ],

time: 148 us -> 110 us (0.74)
  the two profiles are of different devices: /device:TPU:113 before, /device:TPU:8 now
where the time goes in v2:
time: 110 us
  Pallas kernels  104 us (95%)
  local copies, waits for them, and re-layouts  4.74 us (4%)
    pallas_call x1, Pallas kernels, body(): pl.pallas_call(functools.partial(kernel, factor), out_shape=(jax.ShapeDty...  104 us
    unnamed x5, local copies, waits for them, and re-layouts  4.74 us

profile of v2, /device:TPU:8, one launch (start us, length us, event | category | flops | bytes accessed | tf_op | source)
XLA Modules:
  0.0 109.9 jit_solution(12554642151855909646)
XLA Ops:
  0.6 104.5 %swiglu_backward.1 = (bf16[256,256]{1,0:T(8,128)(2,1)}, bf16[128,3584]{1,0:T(8,128)(2,1)}, bf16[128,3584]{1,0:T(8,128)(2,1)}) custom-call(bf16[256,256]{1,0:T(8,128)(2,1)} %x_ref.1, bf16[32,3584]{1,0:T(8,128)(2,1)} %h_ref.1, bf16[32,3584]{1,0:T(8,128)(2,1)} %g_ref.1, bf16[32,3584]{1,0:T(8,128)(2,1)} %u_ref.1, bf16[128,3584]{1,0:T(8,128)(2,1)} %wg_ref.1, ...), custom_call_target="tpu_custom_call" | custom-call | flops 7516192768 | bytes 5505024 | tf_op jit(solution)/shard_map/swiglu_backward/pallas_call | solution.py:365
  105.1 1.6 %copy.12 = bf16[256,256]{1,0:T(8,128)(2,1)} copy(bf16[256,256]{1,0:T(8,128)(2,1)} %get-tuple-element.6) | data formatting | bytes 262144
  106.7 0.0 copy-start
  106.7 2.2 %copy.13 = bf16[128,3584]{1,0:T(8,128)(2,1)} copy(bf16[128,3584]{1,0:T(8,128)(2,1)} %get-tuple-element.7) | data formatting | bytes 1835008
  108.9 0.0 copy-done
  108.9 0.9 copy.14
Async XLA Ops:
  106.7 2.2 %copy-start = (bf16[128,3584]{1,0:T(8,128)(2,1)S(1)}, bf16[128,3584]{1,0:T(8,128)(2,1)}, u32[]{:S(2)}) copy-start(bf16[128,3584]{1,0:T(8,128)(2,1)} %get-tuple-element.8) | copy-start | bytes 2752516

commit v3 on v2

--- a/solution.py
+++ b/solution.py
@@ -74,14 +74,21 @@
     greet(down)
     greet(pair)
 
+    for k in range(NY):
+
+        @pl.when(jnp.logical_or(y != zl, y != k))
+        def _():
+            greet(dev(x, k, zh * NZL + y, c))
+
+    greetings = (NX - 1) + (NY - 1) + 3 + NZL
+
     @pl.when(on_diag)
     def _():
-        pl.semaphore_wait(barrier, (NX - 1) + (NY - 1) + 3)
+        pl.semaphore_wait(barrier, greetings - 1)
 
     @pl.when(jnp.logical_not(on_diag))
     def _():
-        greet(swapped)
-        pl.semaphore_wait(barrier, (NX - 1) + (NY - 1) + 4)
+        pl.semaphore_wait(barrier, greetings)
 
     for q in range(NX):
         part = slice(q * fq, (q + 1) * fq)
@@ -161,9 +168,11 @@
             ring_landed(gu, d, s - 1, part_of(d, j))
             ring_send(gu, d, s, part_of(d, j)).start()
 
-    def ring_end(gu):
+    def ring_near_end(gu):
         for d in range(2):
             ring_landed(gu, d, last - 1, part_of(d, 1))
+
+    def ring_end(gu):
         for d in range(2):
             ring_landed(gu, d, last, part_of(d, 0))
 
@@ -199,10 +208,10 @@
     def dw_pair(gu, i):
         return remote(dws.at[gu, i], dwr.at[gu, i], ec_s.at[gu, i], ec_r.at[gu, i], pair)
 
-    def dw_compute(gu):
+    def dw_compute(gu, first=0, end=NX):
         tokens = gbuf.at[gu]
 
-        @pl.loop(0, NX)
+        @pl.loop(first, end)
         def _(i):
             lhs = xbuf[aligned(i, dc, dc), :]
             rhs = tokens[...].reshape(NZ * shard, fq)
@@ -221,12 +230,12 @@
             else:
                 pltpu.make_async_copy(dwf.at[gu, i], dw_out(gu, x), eo_r.at[gu, x]).start()
 
-    def dx_parts(p, d_zh, d_zl):
-        return dxs.at[p], dxr.at[y, d_zh]
+    def dx_rows(p, k):
+        return dxs.at[p, aligned(k, rows, rows), :]
 
     def dx_shard(zz):
         zz = zz % NZ
-        p, j, owner = place(zz), zz // NZL, zz % NZL
+        p = place(zz)
 
         @pl.loop(0, NX)
         def _(i):
@@ -238,18 +247,54 @@
             )
             dxs[p, :, columns] = total.astype(BF16)
 
-        @pl.when(owner == y)
-        def _():
-            pltpu.make_async_copy(dxs.at[p], dxr.at[y, j], dy_r.at[y, j]).start()
-
-        @pl.when(owner != y)
-        def _():
-            remote(dxs.at[p], dxr.at[y, j], dy_s.at[p], dy_r.at[y, j], dev(x, owner, z, c)).start()
+        pltpu.make_async_copy(dx_rows(p, y), dxr.at[y, p], dy_r.at[p, y]).start()
+        for k in range(1, NY):
+            remote(dx_rows(p, ys[k]), dxr.at[y, p], dy_s.at[p, k], dy_r.at[p, y], dev(x, ys[k], z, c)).start()
 
     def w_end():
         for gu in range(2):
             for i in range(NX):
                 landed(w_rows(gu, i, 1 - c), wc_r.at[gu, i])
+
+    def dx_sum(*shards):
+        for zz in shards:
+            p = place(zz)
+            for i in range(NY):
+                landed(dxr.at[i, p], dy_r.at[p, i])
+            total = dxr[0, p].astype(F32)
+            for k in range(1, NY):
+                total = total + dxr[k, p].astype(F32)
+            for i in range(NX):
+                dxp[i, p] = total[:, i * dc:(i + 1) * dc].astype(BF16)
+            pltpu.make_async_copy(dxp.at[x, p], dxq.at[x, p], dq_r.at[p, x]).start()
+            for k in range(1, NX):
+                remote(dxp.at[xs[k], p], dxq.at[x, p], dq_s.at[p, k], dq_r.at[p, x], dev(xs[k], y, z, c)).start()
+
+    def dx_out(*shards):
+        for zz in shards:
+            zz = zz % NZ
+            p, j, owner = place(zz), zz // NZL, zz % NZL
+            for i in range(NX):
+                landed(dxq.at[i, p], dq_r.at[p, i])
+            total = dxq[0, p].astype(F32)
+            for k in range(1, NX):
+                total = total + dxq[k, p].astype(F32)
+            dxo[p] = total.astype(BF16)
+            target = dx_ref.at[aligned(y * NZH + j, rows, rows), :]
+            stays = jnp.logical_and(on_diag, owner == zl)
+
+            @pl.when(stays)
+            def _():
+                pltpu.make_async_copy(dxo.at[p], target, do_r.at[y, j]).start()
+
+            @pl.when(jnp.logical_not(stays))
+            def _():
+                remote(dxo.at[p], target, do_s.at[p], do_r.at[y, j], dev(x, zl, zh * NZL + owner, c)).start()
+
+    def dx_end():
+        for i in range(NY):
+            for j in range(NZH):
+                landed(dx_ref.at[pl.ds((i * NZH + j) * rows, rows), :], do_r.at[i, j])
 
     for i in range(NX):
         landed(gbuf.at[:, mine, pl.ds(i * rows, rows), :], ga_r.at[i])
@@ -265,6 +310,7 @@
     ring_step(0, 2, 1)
     ring_step(0, 3, 0)
     ring_first(1)
+    ring_near_end(0)
     ring_end(0)
     ring_step(1, 1, 0)
     ring_step(1, 1, 1)
@@ -281,45 +327,18 @@
     ring_step(1, 3, 0)
     dx_shard(z + NZ - 2)
     dx_shard(z + 2)
-    ring_end(1)
+    ring_near_end(1)
     dx_shard(z + NZ - 3)
     dx_shard(z + 3)
+    dx_sum(z, z + NZ - 1, z + 1, z + NZ - 2, z + 2)
+    ring_end(1)
     dx_shard(z + 4)
     dw_compute(1)
+    dx_sum(z + NZ - 3, z + 3, z + 4)
+    dx_out(z, z + NZ - 1, z + 1, z + NZ - 2, z + 2)
     dw_finish(1)
-
-    for i in range(NY):
-        for j in range(NZH):
-            landed(dxr.at[i, j], dy_r.at[i, j])
-    for i in range(NX):
-        columns = slice(i * dc, (i + 1) * dc)
-        total = dxr[0, :, :, columns].astype(F32)
-        for k in range(1, NY):
-            total = total + dxr[k, :, :, columns].astype(F32)
-        dxp[i] = total.astype(BF16)
-
-    pltpu.make_async_copy(dxp.at[x], dxq.at[x], dq_r.at[x]).start()
-    for k in range(1, NX):
-        remote(dxp.at[xs[k]], dxq.at[x], dq_s.at[k], dq_r.at[x], dev(xs[k], y, z, c)).start()
-    for i in range(NX):
-        landed(dxq.at[i], dq_r.at[i])
-    for j in range(NZH):
-        for i in range(NX):
-            part = slice(i * rows, (i + 1) * rows)
-            total = dxq[0, j, part, :].astype(F32)
-            for k in range(1, NX):
-                total = total + dxq[k, j, part, :].astype(F32)
-            dxo[(i * NZH + j) * rows:(i * NZH + j + 1) * rows, :] = total.astype(BF16)
-
-    @pl.when(on_diag)
-    def _():
-        pltpu.make_async_copy(dxo, dx_ref, do_r).start()
-
-    @pl.when(jnp.logical_not(on_diag))
-    def _():
-        remote(dxo, dx_ref, do_s, do_r, swapped).start()
-
-    landed(dx_ref, do_r)
+    dx_out(z + NZ - 3, z + 3, z + 4)
+    dx_end()
 
     for gu in range(2):
         for i in range(NX):
@@ -329,7 +348,9 @@
         sent(x_piece(x, y), xc_s.at[k])
         for i in range(NX):
             sent(x_piece(i, y), xb_s.at[i, k])
-        sent(dxp.at[xs[k]], dq_s.at[k])
+        for p in range(NZ):
+            sent(dx_rows(p, ys[k]), dy_s.at[p, k])
+            sent(dxp.at[xs[k], p], dq_s.at[p, k])
         for gu in range(2):
             sent(w_src(gu, xs[k]), wa_s.at[gu, k])
             sent(dwf.at[gu, xs[k]], eo_s.at[gu, k])
@@ -337,7 +358,6 @@
     @pl.when(jnp.logical_not(on_diag))
     def _():
         sent(xt0, xa_s)
-        sent(dxo, do_s)
 
     for gu in range(2):
         for i in range(NX):
@@ -349,9 +369,9 @@
                     ring_send(gu, d, s, part_of(d, j)).wait_send()
     for p in range(NZ):
 
-        @pl.when(p // NZH != y)
+        @pl.when(jnp.logical_not(jnp.logical_and(on_diag, p // NZH == zl)))
         def _():
-            sent(dxs.at[p], dy_s.at[p])
+            sent(dxo.at[p], do_s.at[p])
 
 
 def body(inputs, hidden_grad, gate_pre, up_pre, gate_weight, up_weight):
@@ -378,10 +398,10 @@
             pltpu.VMEM((dc, NZH * shard), BF16),
             pltpu.VMEM((columns, tokens), BF16),
             pltpu.VMEM((NZ, shard, columns), BF16),
-            pltpu.VMEM((NY, NZH, shard, columns), BF16),
-            pltpu.VMEM((NX, NZH, shard, dc), BF16),
-            pltpu.VMEM((NX, NZH, shard, dc), BF16),
-            pltpu.VMEM((NZH * shard, dc), BF16),
+            pltpu.VMEM((NY, NZ, rows, columns), BF16),
+            pltpu.VMEM((NX, NZ, rows, dc), BF16),
+            pltpu.VMEM((NX, NZ, rows, dc), BF16),
+            pltpu.VMEM((NZ, rows, dc), BF16),
             pltpu.VMEM((2, NX, dc, fq), F32),
             pltpu.VMEM((2, NX, wr, fq), BF16),
             pltpu.VMEM((2, NX, wr, fq), BF16),
@@ -393,9 +413,9 @@
             dma, dma,
             dma((NX, NY)), dma((NX, NY)),
             dma((NX,)), dma((NX,)),
+            dma((NZ, NY)), dma((NZ, NY)),
+            dma((NZ, NX)), dma((NZ, NX)),
             dma((NZ,)), dma((NY, NZH)),
-            dma((NX,)), dma((NX,)),
-            dma, dma,
             dma((2, NX)), dma((2, NX)),
             dma((2, NX)), dma((2, NX)),
         ],

time: 110 us -> 104 us (0.945)
  the two profiles are of different devices: /device:TPU:8 before, /device:TPU:2 now
where the time goes in v3:
time: 104 us
  Pallas kernels  98.3 us (95%)
  local copies, waits for them, and re-layouts  4.74 us (5%)
    pallas_call x1, Pallas kernels, body(): pl.pallas_call(functools.partial(kernel, factor), out_shape=(jax.ShapeDty...  98.3 us
    unnamed x5, local copies, waits for them, and re-layouts  4.74 us

profile of v3, /device:TPU:2, one launch (start us, length us, event | category | flops | bytes accessed | tf_op | source)
XLA Modules:
  0.0 103.6 jit_solution(5047177520166685201)
XLA Ops:
  0.6 98.3 %swiglu_backward.1 = (bf16[256,256]{1,0:T(8,128)(2,1)}, bf16[128,3584]{1,0:T(8,128)(2,1)}, bf16[128,3584]{1,0:T(8,128)(2,1)}) custom-call(bf16[256,256]{1,0:T(8,128)(2,1)} %x_ref.1, bf16[32,3584]{1,0:T(8,128)(2,1)} %h_ref.1, bf16[32,3584]{1,0:T(8,128)(2,1)} %g_ref.1, bf16[32,3584]{1,0:T(8,128)(2,1)} %u_ref.1, bf16[128,3584]{1,0:T(8,128)(2,1)} %wg_ref.1, ...), custom_call_target="tpu_custom_call" | custom-call | flops 7516192768 | bytes 5505024 | tf_op jit(solution)/shard_map/swiglu_backward/pallas_call | solution.py:385
  98.9 1.6 %copy.12 = bf16[256,256]{1,0:T(8,128)(2,1)} copy(bf16[256,256]{1,0:T(8,128)(2,1)} %get-tuple-element.6) | data formatting | bytes 262144
  100.5 0.0 copy-start
  100.5 2.2 %copy.13 = bf16[128,3584]{1,0:T(8,128)(2,1)} copy(bf16[128,3584]{1,0:T(8,128)(2,1)} %get-tuple-element.7) | data formatting | bytes 1835008
  102.7 0.0 copy-done
  102.7 0.9 copy.14
Async XLA Ops:
  100.5 2.2 %copy-start = (bf16[128,3584]{1,0:T(8,128)(2,1)S(1)}, bf16[128,3584]{1,0:T(8,128)(2,1)}, u32[]{:S(2)}) copy-start(bf16[128,3584]{1,0:T(8,128)(2,1)} %get-tuple-element.8) | copy-start | bytes 2752516

commit v4 on v3

--- a/solution.py
+++ b/solution.py
@@ -299,11 +299,11 @@
     for i in range(NX):
         landed(gbuf.at[:, mine, pl.ds(i * rows, rows), :], ga_r.at[i])
     ring_first(0)
+    x_start()
     w_start(0)
-    x_start()
     ring_step(0, 1, 0)
+    x_forward()
     ring_step(0, 1, 1)
-    x_forward()
     w_start(1)
     ring_step(0, 2, 0)
     w_forward(0)

time: 104 us -> 106 us (1.019)
  Pallas kernels: 98.3 us -> 100 us
    pallas_call x1, Pallas kernels: 98.3 us -> 100 us  [body(): pl.pallas_call(functools.partial(kernel, factor), out_shape=(jax.ShapeDty...]
where the time goes in v4:
time: 106 us
  Pallas kernels  100 us (94%)
  local copies, waits for them, and re-layouts  4.74 us (4%)
    pallas_call x1, Pallas kernels, body(): pl.pallas_call(functools.partial(kernel, factor), out_shape=(jax.ShapeDty...  100 us
    unnamed x5, local copies, waits for them, and re-layouts  4.74 us

profile of v4, /device:TPU:2, one launch (start us, length us, event | category | flops | bytes accessed | tf_op | source)
XLA Modules:
  0.0 105.6 jit_solution(6404995041887456201)
XLA Ops:
  0.6 100.2 %swiglu_backward.1 = (bf16[256,256]{1,0:T(8,128)(2,1)}, bf16[128,3584]{1,0:T(8,128)(2,1)}, bf16[128,3584]{1,0:T(8,128)(2,1)}) custom-call(bf16[256,256]{1,0:T(8,128)(2,1)} %x_ref.1, bf16[32,3584]{1,0:T(8,128)(2,1)} %h_ref.1, bf16[32,3584]{1,0:T(8,128)(2,1)} %g_ref.1, bf16[32,3584]{1,0:T(8,128)(2,1)} %u_ref.1, bf16[128,3584]{1,0:T(8,128)(2,1)} %wg_ref.1, ...), custom_call_target="tpu_custom_call" | custom-call | flops 7516192768 | bytes 5505024 | tf_op jit(solution)/shard_map/swiglu_backward/pallas_call | solution.py:385
  100.8 1.6 %copy.12 = bf16[256,256]{1,0:T(8,128)(2,1)} copy(bf16[256,256]{1,0:T(8,128)(2,1)} %get-tuple-element.6) | data formatting | bytes 262144
  102.4 0.0 copy-start
  102.4 2.2 %copy.13 = bf16[128,3584]{1,0:T(8,128)(2,1)} copy(bf16[128,3584]{1,0:T(8,128)(2,1)} %get-tuple-element.7) | data formatting | bytes 1835008
  104.6 0.0 copy-done
  104.6 0.9 copy.14
Async XLA Ops:
  102.4 2.2 %copy-start = (bf16[128,3584]{1,0:T(8,128)(2,1)S(1)}, bf16[128,3584]{1,0:T(8,128)(2,1)}, u32[]{:S(2)}) copy-start(bf16[128,3584]{1,0:T(8,128)(2,1)} %get-tuple-element.8) | copy-start | bytes 2752516

commit v5 on v3

--- a/solution.py
+++ b/solution.py
@@ -330,9 +330,9 @@
     ring_near_end(1)
     dx_shard(z + NZ - 3)
     dx_shard(z + 3)
-    dx_sum(z, z + NZ - 1, z + 1, z + NZ - 2, z + 2)
     ring_end(1)
     dx_shard(z + 4)
+    dx_sum(z, z + NZ - 1, z + 1, z + NZ - 2, z + 2)
     dw_compute(1)
     dx_sum(z + NZ - 3, z + 3, z + 4)
     dx_out(z, z + NZ - 1, z + 1, z + NZ - 2, z + 2)

time: 104 us -> 104 us (level)
  no operation moved by 1% of the time
where the time goes in v5:
time: 104 us
  Pallas kernels  98.4 us (95%)
  local copies, waits for them, and re-layouts  4.74 us (5%)
    pallas_call x1, Pallas kernels, body(): pl.pallas_call(functools.partial(kernel, factor), out_shape=(jax.ShapeDty...  98.4 us
    unnamed x5, local copies, waits for them, and re-layouts  4.74 us

profile of v5, /device:TPU:2, one launch (start us, length us, event | category | flops | bytes accessed | tf_op | source)
XLA Modules:
  0.0 103.8 jit_solution(11848808871715772214)
XLA Ops:
  0.6 98.4 %swiglu_backward.1 = (bf16[256,256]{1,0:T(8,128)(2,1)}, bf16[128,3584]{1,0:T(8,128)(2,1)}, bf16[128,3584]{1,0:T(8,128)(2,1)}) custom-call(bf16[256,256]{1,0:T(8,128)(2,1)} %x_ref.1, bf16[32,3584]{1,0:T(8,128)(2,1)} %h_ref.1, bf16[32,3584]{1,0:T(8,128)(2,1)} %g_ref.1, bf16[32,3584]{1,0:T(8,128)(2,1)} %u_ref.1, bf16[128,3584]{1,0:T(8,128)(2,1)} %wg_ref.1, ...), custom_call_target="tpu_custom_call" | custom-call | flops 7516192768 | bytes 5505024 | tf_op jit(solution)/shard_map/swiglu_backward/pallas_call | solution.py:385
  99.0 1.6 %copy.12 = bf16[256,256]{1,0:T(8,128)(2,1)} copy(bf16[256,256]{1,0:T(8,128)(2,1)} %get-tuple-element.6) | data formatting | bytes 262144
  100.6 0.0 copy-start
  100.6 2.2 %copy.13 = bf16[128,3584]{1,0:T(8,128)(2,1)} copy(bf16[128,3584]{1,0:T(8,128)(2,1)} %get-tuple-element.7) | data formatting | bytes 1835008
  102.8 0.0 copy-done
  102.8 0.9 copy.14
Async XLA Ops:
  100.6 2.2 %copy-start = (bf16[128,3584]{1,0:T(8,128)(2,1)S(1)}, bf16[128,3584]{1,0:T(8,128)(2,1)}, u32[]{:S(2)}) copy-start(bf16[128,3584]{1,0:T(8,128)(2,1)} %get-tuple-element.8) | copy-start | bytes 2752516
